TPU v7x, 32 devices: a whole 2x2x4 slice. The times are simulated.
32 devices in a mesh: rep: 2 (over y), sec: 16 (over z, x, core).
Axes of the slice: x: 2, y: 2, z: 4, core: 2. Of those that a mesh axis runs over, the one named last changes fastest.
Arguments:
- wavefunction: bfloat16 [32, 312, 312], P(('rep', 'sec')), parts along dimension 0, may hold values from -21 to 21
- left_blocks: bfloat16 [28, 32, 312, 312], P(None, ('rep', 'sec')), parts along dimension 1, may hold values from -0.26 to 0.56
- right_blocks: bfloat16 [28, 32, 312, 312], P(None, ('rep', 'sec')), parts along dimension 1, may hold values from -0.0505 to 0.111
- diagonal: float32 [128, 78, 312], P(('rep', 'sec')), parts along dimension 0, may hold values from 0.5 to 6
- target_sector: int32 [56, 16], P('rep'), parts along dimension 0, may hold values from 0 to 15, as said below
- slot_sector: int32 [32], P('rep'), parts along dimension 0, may hold values from 0 to 15, as said below
- widths: int32 [32], P('rep'), parts along dimension 0, may hold values from 64 to 312, as said below
Outputs:
- residual: bfloat16 [128, 78, 312], P(('rep', 'sec')), parts along dimension 0
- quotient: float32 [2], P('rep'), parts along dimension 0
There are 2 independent parts, one for each index of `rep`. A program takes and returns all parts, laid end to end along the dimension named above; each array names one. Nothing has to cross between parts.
Inputs may be any that keep to these rules, and one draw needn't show every extreme that they name: `slot_sector`: a permutation: each sector is held by exactly one slot. `target_sector`: for each term a permutation of the sectors; slots form groups of 4 consecutive indices; for every source slot the terms that lead its sector into one group number at most 8, into its own group at most 7, and every source slot reaches that bound in its own group. `widths`: both 64 and 312 occur.
All inputs are finite; a program needn't handle non-finite values.
Results may differ from a plain program's by a relative error of at most 0.0047.
Values may be sent and summed in bfloat16 or wider, within the bound.
A program may use at most 128 MiB of HBM per device.

v0:
```python
import jax
import jax.numpy as jnp
from jax import lax
from jax.sharding import PartitionSpec as P

PIECES = 4


def earlier_same(labels):
    count = labels.shape[-1]
    same_label = labels[..., :, None] == labels[..., None, :]
    earlier = jnp.arange(count)[None, :] < jnp.arange(count)[:, None]
    return jnp.sum(jnp.logical_and(same_label, earlier).astype(jnp.int32), axis=-1)


def shards(wavefunction, left_blocks, right_blocks, diagonal, target_sector, slot_sector, widths):
    owners = lax.axis_size("sec")
    own_index = lax.axis_index("sec")
    term_count = left_blocks.shape[0]
    block_width = wavefunction.shape[1]
    piece_rows = block_width // PIECES
    groups = owners // PIECES
    capacity = (term_count + groups) // groups
    item_count = term_count + 1
    positions = jnp.arange(owners, dtype=jnp.int32)
    slot_of = jnp.zeros((owners,), jnp.int32).at[slot_sector].set(positions)
    targets = slot_of[target_sector[:, slot_sector]]
    live_width = widths[slot_sector]
    column_ids = jnp.arange(block_width, dtype=jnp.int32)
    own_keep = column_ids < live_width[own_index]
    live_block = wavefunction[0] * jnp.logical_and(own_keep[:, None], own_keep[None, :]).astype(
        wavefunction.dtype
    )
    item_slots = jnp.concatenate([jnp.reshape(own_index, (1,)), targets[:, own_index]])
    item_groups = item_slots // PIECES
    item_rank = earlier_same(item_groups)
    destination = jnp.arange(PIECES, dtype=jnp.int32)[None, :] * groups + item_groups[:, None]
    rank_grid = jnp.broadcast_to(item_rank[:, None], (item_count, PIECES))
    half_done = jnp.einsum(
        "tij,jk->tik", left_blocks[:, 0], live_block, preferred_element_type=jnp.float32
    ).astype(jnp.bfloat16)
    term_blocks = jnp.einsum(
        "tik,tlk->til", half_done, right_blocks[:, 0], preferred_element_type=jnp.float32
    ).astype(jnp.bfloat16)
    pieces = jnp.reshape(
        jnp.concatenate([live_block[None], term_blocks]),
        (item_count, PIECES, piece_rows, block_width),
    )
    outgoing = (
        jnp.zeros((owners, capacity, piece_rows, block_width), jnp.bfloat16)
        .at[destination, rank_grid]
        .set(pieces)
    )
    received = lax.all_to_all(outgoing, "sec", split_axis=0, concat_axis=0, tiled=True)
    my_piece = own_index // groups
    my_group = own_index % groups
    all_slots = jnp.concatenate([positions[:, None], jnp.transpose(targets)], axis=1)
    all_groups = all_slots // PIECES
    all_rank = earlier_same(all_groups)
    is_mine = all_groups == my_group
    rank_hit = jnp.logical_and(
        all_rank[:, :, None] == jnp.arange(capacity, dtype=jnp.int32)[None, None, :],
        is_mine[:, :, None],
    )
    place_hit = (
        (all_slots % PIECES)[:, :, None] == jnp.arange(PIECES, dtype=jnp.int32)[None, None, :]
    ).astype(jnp.float32)
    is_live = (jnp.arange(item_count) == 0)[None, :, None]
    live_weight = jnp.einsum(
        "smc,smp->scp", jnp.logical_and(rank_hit, is_live).astype(jnp.float32), place_hit
    )
    term_weight = jnp.einsum(
        "smc,smp->scp",
        jnp.logical_and(rank_hit, jnp.logical_not(is_live)).astype(jnp.float32),
        place_hit,
    )
    live_pieces = jnp.einsum(
        "scp,scab->pab",
        live_weight.astype(jnp.bfloat16),
        received,
        preferred_element_type=jnp.float32,
    )
    applied = jnp.einsum(
        "scp,scab->pab",
        term_weight.astype(jnp.bfloat16),
        received,
        preferred_element_type=jnp.float32,
    )
    my_slots = my_group * PIECES + jnp.arange(PIECES, dtype=jnp.int32)
    widths_here = live_width[my_slots]
    row_global = my_piece * piece_rows + jnp.arange(piece_rows, dtype=jnp.int32)
    keep_piece_rows = row_global[None, :] < widths_here[:, None]
    keep_piece_cols = column_ids[None, :] < widths_here[:, None]
    piece_box = jnp.logical_and(keep_piece_rows[:, :, None], keep_piece_cols[:, None, :]).astype(
        jnp.float32
    )
    product = diagonal * live_pieces + applied
    correlation_local = jnp.sum(live_pieces * product)
    correlation, squares = lax.psum((correlation_local, jnp.sum(live_pieces * live_pieces)), "sec")
    quotient = correlation / squares
    residual = ((product - quotient * live_pieces) * piece_box).astype(jnp.bfloat16)
    return (residual, jnp.reshape(quotient, (1,)))


def solution(mesh):
    in_specs = (
        P(("rep", "sec"), None, None),
        P(None, ("rep", "sec"), None, None),
        P(None, ("rep", "sec"), None, None),
        P(("rep", "sec"), None, None),
        P("rep", None),
        P("rep"),
        P("rep"),
    )
    out_specs = (P(("rep", "sec"), None, None), P("rep"))
    return jax.shard_map(shards, mesh=mesh, in_specs=in_specs, out_specs=out_specs, check_vma=False)
```

profile of v0, /device:TPU:0, one launch (start us, length us, event | category | flops | bytes accessed | tf_op | source)
XLA Modules:
  0.0 297.1 jit_solution(6299782499776952255)
XLA Ops:
  0.6 0.0 copy-start
  0.6 0.7 compare_select_fusion.3
  1.3 0.0 copy-done
  1.3 0.6 gather_fusion.2
  1.9 0.1 copy.46
  2.0 0.1 reshape.620
  2.1 0.6 scatter_custom_fusion
  2.7 0.0 copy-start.1
  2.7 0.0 copy-start.3
  2.7 3.0 %gather_fusion.3 = s32[448]{0:T(512)S(1)} fusion(s32[16]{0:T(128)S(1)} %scatter_custom_fusion, s32[1024]{0:T(1024)S(1)} %pad_clamp_fusion), kind=kCustom, calls=%fused_computation.3 | custom fusion | bytes 5376 | tf_op jit(solution)/shard_map/gather | solution.py:27
  5.8 0.1 reshape.619
  5.8 0.2 dynamic-slice_reduce_fusion
  6.0 0.1 and_select_fusion.1
  6.1 0.2 convert_reduce_fusion.1
  6.3 0.1 fusion.32
  6.4 0.1 reshape.634
  6.5 0.0 copy-done.1
  6.5 0.7 gather_fusion
  7.2 0.6 dynamic_slice.7
  7.8 0.6 iota_compare_fusion.8
  8.5 0.0 copy-done.3
  8.5 0.1 and_select_fusion
  8.6 0.1 concatenate.97
  8.7 13.6 %convolution_convert_fusion = bf16[28,312,312]{2,1,0:T(8,128)(2,1)} fusion(bf16[28,1,312,312]{3,2,1,0:T(8,128)(2,1)} %param.9, bf16[28,1,312,312]{3,2,1,0:T(8,128)(2,1)} %param.8, bf16[1,312,312]{2,1,0:T(8,128)(2,1)S(1)} %and_select_fusion), kind=kOutput, calls=%fused_computation.7 | convolution fusion | flops 3407040000 | bytes 16548480 | tf_op jit(solution)/shard_map/tik,tlk->til/dot_general | solution.py:42
  22.3 10.0 %concatenate.98 = bf16[28,4,78,312]{3,2,1,0:T(8,128)(2,1)} reshape(bf16[28,312,312]{2,1,0:T(8,128)(2,1)} %convolution_convert_fusion) | data formatting | bytes 10902528 | tf_op jit(solution)/shard_map/concatenate | solution.py:46
  32.3 7.2 %pad_maximum_fusion = bf16[29,4,78,312]{3,2,1,0:T(8,128)(2,1)} fusion(bf16[28,4,78,312]{3,2,1,0:T(8,128)(2,1)} %concatenate.98, bf16[1,4,78,312]{3,2,1,0:T(8,128)(2,1)S(1)} %concatenate.97), kind=kLoop, calls=%fused_computation.6 | loop fusion | flops 2822976 | bytes 11291904 | tf_op jit(solution)/shard_map/concatenate | solution.py:46
  39.5 4.1 %broadcast_in_dim.11 = bf16[16,8,78,312]{3,2,1,0:T(8,128)(2,1)} broadcast(bf16[]{:T(256)} %constant.76.clone.1), dimensions={} | broadcast | bytes 6230018 | tf_op jit(solution)/shard_map/broadcast_in_dim | solution.py:50
  43.6 24.2 %scatter_fusion = bf16[16,8,78,312]{3,2,1,0:T(8,128)(2,1)} fusion(bf16[16,8,78,312]{3,2,1,0:T(8,128)(2,1)} %broadcast_in_dim.11, s32[116]{0:T(128)S(1)} %reshape.634, bf16[116,78,312]{2,1,0:T(8,128)(2,1)} %bitcast.62), kind=kCustom, calls=%fused_computation.5 | custom fusion | bytes 16938784 | tf_op jit(solution)/shard_map/scatter | solution.py:52
  67.8 8.2 %copy.52 = bf16[16,8,78,312]{3,1,2,0:T(8,128)(2,1)} copy(bf16[16,8,78,312]{3,2,1,0:T(8,128)(2,1)} %scatter_fusion) | data formatting | bytes 12460032 | tf_op jit(solution)/shard_map/scatter | solution.py:52
  76.0 7.4 %all-to-all-start = ((bf16[16,8,78,312]{3,1,2,0:T(8,128)(2,1)}), bf16[16,8,78,312]{3,1,2,0:T(8,128)(2,1)}, u32[]{:S(2)}, u32[]{:S(2)}) async-start(bf16[16,8,78,312]{3,1,2,0:T(8,128)(2,1)} %copy.52), calls=%async_computation | async-start | bytes 15335424 | tf_op jit(solution)/shard_map/all_to_all | solution.py:54
  83.4 0.0 copy-start.2
  83.4 0.1 copy.47
  83.5 0.1 broadcast_compare_fusion.1
  83.6 0.1 copy.48
  83.7 0.7 convert_reduce_fusion
  84.4 0.1 copy.49
  84.5 0.6 gather_fusion.1
  85.2 0.1 add_select_fusion
  85.2 0.1 iota_compare_fusion.7
  85.3 0.1 broadcast_compare_fusion
  85.4 136.2 %all-to-all-done = bf16[16,8,78,312]{3,1,2,0:T(8,128)(2,1)} async-done(((bf16[16,8,78,312]{3,1,2,0:T(8,128)(2,1)}), bf16[16,8,78,312]{3,1,2,0:T(8,128)(2,1)}, u32[]{:S(2)}, u32[]{:S(2)}) %all-to-all-start) | async-done | bytes 6230048 | tf_op jit(solution)/shard_map/all_to_all | solution.py:54
  221.6 4.5 %convolution_bitcast_fusion.1 = f32[4,78,312]{2,0,1:T(4,128)S(1)} fusion(bf16[16,8,78,312]{3,1,2,0:T(8,128)(2,1)} %all-to-all-done, s32[16,29]{1,0:T(8,128)S(1)} %copy.49, pred[29]{0:T(512)(128)(4,1)S(1)} %iota_compare_fusion.9, pred[16,29]{1,0:T(8,128)(4,1)S(1)} %get-tuple-element.6, s32[16,29]{1,0:T(8,128)S(1)} %add_select_fusion), kind=kOutput, calls=%fused_computation.13 | convolution fusion | flops 24963264 | bytes 6623597 | tf_op jit(solution)/shard_map/scp,scab->pab/dot_general | solution.py:77
  226.0 0.0 copy-done.2
  226.1 5.3 %multiply_reduce_fusion = (f32[]{:T(128)}, f32[]{:T(128)}, f32[4,78,312]{2,0,1:T(4,128)S(1)}) fusion(f32[4,78,312]{2,0,1:T(4,128)S(1)} %convolution_bitcast_fusion.1, bf16[16,8,78,312]{3,1,2,0:T(8,128)(2,1)} %all-to-all-done, s32[16,29]{1,0:T(8,128)S(1)} %copy.49, pred[29]{0:T(512)(128)(4,1)S(1)} %fusion.43, pred[16,29]{1,0:T(8,128)(4,1)S(1)} %get-tuple-element.6, ...), kind=kOutput, calls=%fused_computation.20 | convolution fusion | flops 25547328 | bytes 7402357 | tf_op jit(solution)/shard_map/scp,scab->pab/dot_general | solution.py:83
  231.4 62.2 %all-reduce = (f32[]{:T(128)}, f32[]{:T(128)}) all-reduce(f32[]{:T(128)} %get-tuple-element.3, f32[]{:T(128)} %get-tuple-element.2), channel_id=1, replica_groups=mesh['rep'=2,'sec'=16] {'sec'}, use_global_device_ids=true, to_apply=%region_5.6 | all-reduce | flops 2 | bytes 16 | tf_op jit(solution)/shard_map/psum | solution.py:99
  295.0 1.0 select_convert_fusion
  (14 shorter events, 0.1 us)
Async XLA Ops:
  0.6 0.7 copy-start
  2.7 3.8 %copy-start.1 = (s32[16]{0:T(128)S(1)}, s32[16]{0:T(128)}, u32[]{:S(2)}) copy-start(s32[16]{0:T(128)} %param.13) | copy-start | bytes 196
  2.7 5.7 %copy-start.3 = (bf16[1,312,312]{2,1,0:T(8,128)(2,1)S(1)}, bf16[1,312,312]{2,1,0:T(8,128)(2,1)}, u32[]{:S(2)}) copy-start(bf16[1,312,312]{2,1,0:T(8,128)(2,1)} %param.7) | copy-start | bytes 584068
  76.0 145.5 %all-to-all-start = ((bf16[16,8,78,312]{3,1,2,0:T(8,128)(2,1)}), bf16[16,8,78,312]{3,1,2,0:T(8,128)(2,1)}, u32[]{:S(2)}, u32[]{:S(2)}) async-start(bf16[16,8,78,312]{3,1,2,0:T(8,128)(2,1)} %copy.52), calls=%async_computation | async-start | bytes 15335424 | tf_op jit(solution)/shard_map/all_to_all | solution.py:54
  83.4 142.6 %copy-start.2 = (f32[4,78,312]{2,0,1:T(4,128)S(1)}, f32[4,78,312]{2,0,1:T(4,128)}, u32[]{:S(2)}) copy-start(f32[4,78,312]{2,0,1:T(4,128)} %param.10) | copy-start | bytes 1168132
where the time goes:
time: 298 us; the launch traced here: 297 us
  waiting for transfers between devices  136 us (46%)
  blocking collectives  62.2 us (21%)
  local copies, waits for them, and re-layouts  53.5 us (18%)
  matrix products  23.4 us (8%)
  other arithmetic  11 us (4%)
  starting transfers between devices  7.39 us (2%)
  between operations  3.32 us (1%)
    all_to_all x1, waiting for transfers between devices, shards(): lax.all_to_all(outgoing, 'sec', split_axis=0, concat_axis=0, tiled=True)  136 us
    psum x1, blocking collectives, shards(): lax.psum((correlation_local, jnp.sum(live_pieces * live_pieces)), 'sec')  62.2 us
    scatter x2, local copies, waits for them, and re-layouts, shards(): outgoing = jnp.zeros((owners, capacity, piece_rows, block_width), jnp.bfl...  32.4 us
    dot_general x1, matrix products, shards(): jnp.einsum('tik,tlk->til', half_done, right_blocks[:, 0], preferred_eleme...  13.6 us
    concatenate x2, local copies, waits for them, and re-layouts, shards(): jnp.concatenate([live_block[None], term_blocks])  10.1 us
    all_to_all x1, starting transfers between devices, shards(): lax.all_to_all(outgoing, 'sec', split_axis=0, concat_axis=0, tiled=True)  7.39 us
    concatenate x1, other arithmetic, shards(): jnp.concatenate([live_block[None], term_blocks])  7.18 us
  transfers between devices with their start and end apart: 1, of which 1 were waited for; matrix products, arithmetic and copies ran while one was open for 1% of the time, Pallas kernels for 0%

commit v1 on v0

--- a/solution.py
+++ b/solution.py
@@ -1,9 +1,14 @@
+import functools
+
 import jax
 import jax.numpy as jnp
 from jax import lax
+from jax.experimental import pallas as pl
+from jax.experimental.pallas import tpu as pltpu
 from jax.sharding import PartitionSpec as P
 
 PIECES = 4
+MESH = pl.DeviceIdType.MESH
 
 
 def earlier_same(labels):
@@ -13,7 +18,7 @@
     return jnp.sum(jnp.logical_and(same_label, earlier).astype(jnp.int32), axis=-1)
 
 
-def shards(wavefunction, left_blocks, right_blocks, diagonal, target_sector, slot_sector, widths):
+def gathered_shards(wavefunction, left_blocks, right_blocks, diagonal, target_sector, slot_sector, widths):
     owners = lax.axis_size("sec")
     own_index = lax.axis_index("sec")
     term_count = left_blocks.shape[0]
@@ -102,6 +107,351 @@
     return (residual, jnp.reshape(quotient, (1,)))
 
 
+def round_up(value, unit):
+    return (value + unit - 1) // unit * unit
+
+
+def local_kernel(
+    slot_sector, target_sector, widths, wave, left, right, out, live_out,
+    slot_of, lbuf, rbuf, acc, lsem, rsem,
+):
+    terms, width = lbuf.shape[0], lbuf.shape[1]
+    owners = slot_sector.shape[0]
+    me = lax.axis_index("sec")
+    rows = width // PIECES
+    main = width // 128 * 128
+    rest = width - main
+
+    @pl.loop(0, terms)
+    def _(t):
+        pltpu.make_async_copy(left.at[t], lbuf.at[t], lsem.at[t]).start()
+        pltpu.make_async_copy(right.at[t], rbuf.at[t], rsem.at[t]).start()
+
+    @pl.loop(0, owners)
+    def _(d):
+        slot_of[slot_sector[d]] = d
+
+    @pl.loop(0, owners)
+    def _(d):
+        acc[d] = jnp.zeros(acc.shape[1:], acc.dtype)
+
+    sector = slot_sector[me]
+    own_width = widths[sector]
+    row_ids = lax.broadcasted_iota(jnp.int32, (width, width), 0)
+    column_ids = lax.broadcasted_iota(jnp.int32, (width, width), 1)
+    keep = jnp.logical_and(row_ids < own_width, column_ids < own_width)
+    live_wide = jnp.where(keep, wave[0].astype(jnp.float32), 0.0)
+    live = live_wide.astype(jnp.bfloat16)
+    for p in range(PIECES):
+        piece = live_wide[p * rows : (p + 1) * rows].astype(jnp.bfloat16)
+        live_out[p, :rows, :width] = piece
+
+    batch = 4
+
+    @pl.loop(0, terms // batch)
+    def _(step):
+        for b in range(batch):
+            t = step * batch + b
+            pltpu.make_async_copy(left.at[t], lbuf.at[t], lsem.at[t]).wait()
+            pltpu.make_async_copy(right.at[t], rbuf.at[t], rsem.at[t]).wait()
+        blocks = []
+        for b in range(batch):
+            t = step * batch + b
+            half = jnp.dot(lbuf[t], live, preferred_element_type=jnp.float32)
+            blocks.append(
+                lax.dot_general(
+                    half.astype(jnp.bfloat16), rbuf[t], (((1,), (1,)), ((), ())),
+                    preferred_element_type=jnp.float32,
+                )
+            )
+        for b in range(batch):
+            v = slot_of[target_sector[step * batch + b, sector]]
+            acc[v] += blocks[b]
+
+    pad = jnp.zeros((rows, out.shape[-1] - 2 * width), jnp.float32)
+
+    @pl.loop(0, owners // 2)
+    def _(pair):
+        for p in range(PIECES):
+            even = acc[2 * pair, p * rows : (p + 1) * rows, :]
+            odd = acc[2 * pair + 1, p * rows : (p + 1) * rows, :]
+            packed = jnp.concatenate(
+                [even[:, :main], odd[:, :main], even[:, main:], odd[:, main:], pad], axis=1
+            )
+            out[pair // 2, 2 * p + pair % 2, :rows, :] = packed.astype(out.dtype)
+
+
+def reduce_kernel(
+    slot_sector, widths, sums, live_pieces, diagonal, residual, quotient,
+    own, crecv, xrecv, zrecv, lives, diag, product, stats, stats_all,
+    own_sem, diag_sem, self_sem, csend_sem, crecv_sem, xsend_sem, xrecv_sem, zsend_sem, zrecv_sem,
+    lsend_sem, lrecv_sem, ssend_sem, srecv_sem,
+):
+    rep = lax.axis_index("rep")
+    me = lax.axis_index("sec")
+    owners = slot_sector.shape[0]
+    z, x, c = me // 4, (me // 2) % 2, me % 2
+    group = me % 4
+    units = 2 * PIECES
+    rows, width = diag.shape[1], diag.shape[2]
+    main = width // 128 * 128
+    rest = width - main
+    far, near = (1 - x) * 2, x * 2
+
+    def unit_of(i):
+        return ((z + 1 + i // 2) % PIECES) * 2 + i % 2
+
+    def core_copy(which, u):
+        source_group = (far if which == 0 else near) + (1 - c)
+        return pltpu.make_async_remote_copy(
+            src_ref=sums.at[source_group, u], dst_ref=crecv.at[which, u],
+            send_sem=csend_sem.at[which, u], recv_sem=crecv_sem.at[which, u],
+            device_id=(rep, near + z * 4 + (1 - c)), device_id_type=MESH,
+        )
+
+    def x_copy(u):
+        return pltpu.make_async_remote_copy(
+            src_ref=own.at[0, u], dst_ref=xrecv.at[u],
+            send_sem=xsend_sem.at[u], recv_sem=xrecv_sem.at[u],
+            device_id=(rep, z * 4 + far + c), device_id_type=MESH,
+        )
+
+    def z_copy(u, source_z):
+        q = u % 2
+        return pltpu.make_async_remote_copy(
+            src_ref=own.at[1, u], dst_ref=zrecv.at[source_z, q],
+            send_sem=zsend_sem.at[u], recv_sem=zrecv_sem.at[source_z, q],
+            device_id=(rep, (u // 2) * 4 + group), device_id_type=MESH,
+        )
+
+    def live_copy(p, place):
+        return pltpu.make_async_remote_copy(
+            src_ref=live_pieces.at[p], dst_ref=lives.at[place],
+            send_sem=lsend_sem.at[p], recv_sem=lrecv_sem.at[place],
+            device_id=(rep, p * 4 + z), device_id_type=MESH,
+        )
+
+    def stats_copy(other, source):
+        return pltpu.make_async_remote_copy(
+            src_ref=stats, dst_ref=stats_all.at[source],
+            send_sem=ssend_sem.at[other], recv_sem=srecv_sem.at[source],
+            device_id=(rep, other), device_id_type=MESH,
+        )
+
+    own_far = pltpu.make_async_copy(sums.at[far + c], own.at[0], own_sem.at[0])
+    own_near = pltpu.make_async_copy(sums.at[near + c], own.at[1], own_sem.at[1])
+    own_far.start()
+    own_near.start()
+    diag_copy = pltpu.make_async_copy(diagonal, diag, diag_sem)
+    diag_copy.start()
+
+    barrier = pltpu.get_barrier_semaphore()
+
+    @pl.loop(1, owners)
+    def _(d):
+        pl.semaphore_signal(
+            barrier, inc=1, device_id=(rep, (me + d) % owners), device_id_type=MESH
+        )
+
+    pl.semaphore_wait(barrier, owners - 1)
+
+    @pl.loop(0, units)
+    def _(i):
+        core_copy(0, unit_of(i)).start()
+
+    @pl.loop(0, units)
+    def _(i):
+        core_copy(1, unit_of(i)).start()
+
+    self_copy = pltpu.make_async_copy(live_pieces.at[z], lives.at[group], self_sem)
+    for p in range(PIECES):
+
+        @pl.when(p * 4 + z != me)
+        def _():
+            live_copy(p, group).start()
+
+        @pl.when(p * 4 + z == me)
+        def _():
+            self_copy.start()
+
+    own_far.wait()
+
+    @pl.loop(0, units)
+    def _(i):
+        u = unit_of(i)
+        core_copy(0, u).wait_recv()
+        total = own[0, u].astype(jnp.float32) + crecv[0, u].astype(jnp.float32)
+        own[0, u] = total.astype(own.dtype)
+        x_copy(u).start()
+
+    own_near.wait()
+
+    @pl.loop(0, units - 2)
+    def _(i):
+        u = unit_of(i)
+        core_copy(1, u).wait_recv()
+        x_copy(u).wait_recv()
+        total = own[1, u].astype(jnp.float32) + crecv[1, u].astype(jnp.float32)
+        total += xrecv[u].astype(jnp.float32)
+        own[1, u] = total.astype(own.dtype)
+        z_copy(u, z).start()
+
+    for j in range(PIECES):
+        source = group * 4 + j
+
+        @pl.when(source != me)
+        def _():
+            live_copy(0, j).wait_recv()
+
+        @pl.when(source == me)
+        def _():
+            self_copy.wait()
+
+    diag_copy.wait()
+
+    correlation = jnp.zeros((1, width), jnp.float32)
+    squares = jnp.zeros((1, width), jnp.float32)
+    for q in range(2):
+        u = z * 2 + q
+        core_copy(1, u).wait_recv()
+        x_copy(u).wait_recv()
+        total = own[1, u].astype(jnp.float32) + crecv[1, u].astype(jnp.float32)
+        total += xrecv[u].astype(jnp.float32)
+        for d in range(1, PIECES):
+            source_z = (z + d) % PIECES
+            z_copy(q, source_z).wait_recv()
+            total += zrecv[source_z, q].astype(jnp.float32)
+        total = total[:rows]
+        tail = 2 * main
+        for parity in range(2):
+            j = 2 * q + parity
+            applied = jnp.concatenate(
+                [
+                    total[:, parity * main : (parity + 1) * main],
+                    total[:, tail + parity * rest : tail + (parity + 1) * rest],
+                ],
+                axis=1,
+            )
+            live = lives[j, :rows, :width].astype(jnp.float32)
+            block = diag[j] * live + applied
+            product[j] = block
+            correlation += jnp.sum(live * block, axis=0, keepdims=True)
+            squares += jnp.sum(live * live, axis=0, keepdims=True)
+
+    row_ids = lax.broadcasted_iota(jnp.int32, stats.shape, 0)
+    mine = jnp.where(row_ids == 0, jnp.sum(correlation), jnp.sum(squares))
+    stats[...] = mine
+    stats_all[me] = mine
+
+    @pl.loop(1, owners)
+    def _(d):
+        stats_copy((me + d) % owners, me).start()
+
+    @pl.loop(1, owners)
+    def _(d):
+        stats_copy(me, (me + d) % owners).wait_recv()
+
+    whole = stats_all[0]
+    for d in range(1, owners):
+        whole += stats_all[d]
+    ratio = whole[0:1, 0:1] / whole[1:2, 0:1]
+    quotient[...] = jnp.broadcast_to(ratio, quotient.shape)
+    row_ids = lax.broadcasted_iota(jnp.int32, (rows, width), 0) + z * rows
+    column_ids = lax.broadcasted_iota(jnp.int32, (rows, width), 1)
+    for j in range(PIECES):
+        slot_width = widths[slot_sector[group * 4 + j]]
+        keep = jnp.logical_and(row_ids < slot_width, column_ids < slot_width)
+        live = lives[j, :rows, :width].astype(jnp.float32)
+        value = jnp.where(keep, product[j] - ratio * live, 0.0)
+        residual[j] = value.astype(residual.dtype)
+
+    @pl.loop(0, units)
+    def _(u):
+        core_copy(0, u).wait_send()
+        core_copy(1, u).wait_send()
+        x_copy(u).wait_send()
+
+    @pl.loop(0, units - 2)
+    def _(i):
+        z_copy(unit_of(i), z).wait_send()
+
+    for p in range(PIECES):
+
+        @pl.when(p * 4 + z != me)
+        def _():
+            live_copy(p, group).wait_send()
+
+    @pl.loop(1, owners)
+    def _(d):
+        stats_copy((me + d) % owners, me).wait_send()
+
+
+def kernel_shards(
+    wavefunction, left_blocks, right_blocks, diagonal, target_sector, slot_sector, widths
+):
+    terms, _, width, _ = left_blocks.shape
+    owners = slot_sector.shape[0]
+    rows = width // PIECES
+    groups = owners // PIECES
+    units = 2 * PIECES
+    tall = round_up(rows, 16)
+    lanes = round_up(width, 128)
+    packed = round_up(2 * width, 128)
+    smem = pl.BlockSpec(memory_space=pltpu.SMEM)
+    vmem = pl.BlockSpec(memory_space=pltpu.VMEM)
+    hbm = pl.BlockSpec(memory_space=pl.ANY)
+    sums, live_pieces = pl.pallas_call(
+        local_kernel,
+        out_shape=(
+            jax.ShapeDtypeStruct((groups, units, tall, packed), jnp.bfloat16),
+            jax.ShapeDtypeStruct((PIECES, tall, lanes), jnp.bfloat16),
+        ),
+        in_specs=[smem, smem, smem, vmem, hbm, hbm],
+        out_specs=(vmem, vmem),
+        scratch_shapes=[
+            pltpu.SMEM((owners,), jnp.int32),
+            pltpu.VMEM((terms, width, width), jnp.bfloat16),
+            pltpu.VMEM((terms, width, width), jnp.bfloat16),
+            pltpu.VMEM((owners, width, width), jnp.float32),
+            pltpu.SemaphoreType.DMA((terms,)),
+            pltpu.SemaphoreType.DMA((terms,)),
+        ],
+        compiler_params=pltpu.CompilerParams(vmem_limit_bytes=48 << 20),
+        name="local_sums",
+    )(slot_sector, target_sector, widths, wavefunction, left_blocks[:, 0], right_blocks[:, 0])
+    block = (tall, packed)
+    dma = pltpu.SemaphoreType.DMA
+    residual, quotient = pl.pallas_call(
+        reduce_kernel,
+        out_shape=(
+            jax.ShapeDtypeStruct((PIECES, rows, width), jnp.bfloat16),
+            jax.ShapeDtypeStruct((1, 1), jnp.float32),
+        ),
+        in_specs=[smem, smem, hbm, hbm, hbm],
+        out_specs=(vmem, vmem),
+        scratch_shapes=[
+            pltpu.VMEM((2, units, *block), jnp.bfloat16),
+            pltpu.VMEM((2, units, *block), jnp.bfloat16),
+            pltpu.VMEM((units, *block), jnp.bfloat16),
+            pltpu.VMEM((PIECES, 2, *block), jnp.bfloat16),
+            pltpu.VMEM((PIECES, tall, lanes), jnp.bfloat16),
+            pltpu.VMEM((PIECES, rows, width), jnp.float32),
+            pltpu.VMEM((PIECES, rows, width), jnp.float32),
+            pltpu.VMEM((8, 128), jnp.float32),
+            pltpu.VMEM((owners, 8, 128), jnp.float32),
+            dma((2,)), dma, dma,
+            dma((2, units)), dma((2, units)), dma((units,)), dma((units,)),
+            dma((units,)), dma((PIECES, 2)),
+            dma((PIECES,)), dma((PIECES,)), dma((owners,)), dma((owners,)),
+        ],
+        compiler_params=pltpu.CompilerParams(
+            collective_id=0, has_side_effects=True, vmem_limit_bytes=48 << 20
+        ),
+        name="reduce_pieces",
+    )(slot_sector, widths, sums, live_pieces, diagonal)
+    return residual, jnp.reshape(quotient, (1,))
+
+
 def solution(mesh):
     in_specs = (
         P(("rep", "sec"), None, None),
@@ -113,4 +463,6 @@
         P("rep"),
     )
     out_specs = (P(("rep", "sec"), None, None), P("rep"))
+    fast = mesh.shape["sec"] == PIECES * 4
+    shards = kernel_shards if fast else gathered_shards
     return jax.shard_map(shards, mesh=mesh, in_specs=in_specs, out_specs=out_specs, check_vma=False)

time: 298 us -> 64 us (0.21)
  waiting for transfers between devices: 136 us -> 0 us
  blocking collectives: 62.2 us -> 0 us
  Pallas kernels: 0 us -> 56.5 us
  local copies, waits for them, and re-layouts: 53.5 us -> 4.87 us
  matrix products: 23.4 us -> 0 us
  other arithmetic: 11 us -> 0 us
  starting transfers between devices: 7.39 us -> 0 us
    all_to_all x1 -> x0, waiting for transfers between devices: 136 us -> none  [shards(): lax.all_to_all(outgoing, 'sec', split_axis=0, concat_axis=0, tiled=True)]
    psum x1 -> x0, blocking collectives: 62.2 us -> none  [shards(): lax.psum((correlation_local, jnp.sum(live_pieces * live_pieces)), 'sec')]
    pallas_call x0 -> x2, Pallas kernels: none -> 56.5 us  [the longest x1 40.9 us: kernel_shards(): pl.pallas_call(reduce_kernel, out_shape=(jax.ShapeDtypeStruct((PIECES, ro...]
    scatter x3 -> x0, local copies, waits for them, and re-layouts: 33 us -> none  [the longest x2 32.4 us: shards(): outgoing = jnp.zeros((owners, capacity, piece_rows, block_width), jnp.bfl...]
    dot_general x3 -> x0, matrix products: 23.4 us -> none  [the longest x1 13.6 us: shards(): jnp.einsum('tik,tlk->til', half_done, right_blocks[:, 0], preferred_eleme...]
    concatenate x3 -> x0, local copies, waits for them, and re-layouts: 10.2 us -> none  [the longest x2 10.1 us: shards(): jnp.concatenate([live_block[None], term_blocks])]
    all_to_all x1 -> x0, starting transfers between devices: 7.39 us -> none  [shards(): lax.all_to_all(outgoing, 'sec', split_axis=0, concat_axis=0, tiled=True)]
    concatenate x2 -> x0, other arithmetic: 7.27 us -> none  [the longest x1 7.18 us: shards(): jnp.concatenate([live_block[None], term_blocks])]
  transfers between devices with their start and end apart: 1 -> 0, of which waited for: 1 -> 0; matrix products, arithmetic and copies ran while one was open for 1% -> 0% of each run, Pallas kernels for 0% -> 0%
where the time goes in v1:
time: 64 us; the launch traced here: 63.8 us
  Pallas kernels  56.5 us (88%)
  local copies, waits for them, and re-layouts  4.87 us (8%)
  between operations  2.41 us (4%)
    pallas_call x1, Pallas kernels, kernel_shards(): pl.pallas_call(reduce_kernel, out_shape=(jax.ShapeDtypeStruct((PIECES, ro...  40.9 us
    pallas_call x1, Pallas kernels, kernel_shards(): pl.pallas_call(local_kernel, out_shape=(jax.ShapeDtypeStruct((groups, uni...  15.6 us
    unnamed x9, local copies, waits for them, and re-layouts  4.87 us

profile of v1, /device:TPU:0, one launch (start us, length us, event | category | flops | bytes accessed | tf_op | source)
XLA Modules:
  0.0 63.8 jit_solution(2025521837838020429)
XLA Ops:
  0.6 0.8 %copy.9.target_sector = s32[28,16]{1,0:T(8,128)S(1)} copy(s32[28,16]{0,1:T(8,128)} %param.11) | data formatting | bytes 3584 | tf_op args[4]
  1.4 1.1 %copy.10.diagonal = f32[4,78,312]{2,1,0:T(8,128)S(1)} copy(f32[4,78,312]{2,0,1:T(4,128)} %param.10) | data formatting | bytes 778752 | tf_op args[3]
  2.5 0.0 copy-start
  2.5 0.9 %copy-done = bf16[1,312,312]{2,1,0:T(8,128)(2,1)S(1)} copy-done((bf16[1,312,312]{2,1,0:T(8,128)(2,1)S(1)}, bf16[1,312,312]{2,1,0:T(8,128)(2,1)}, u32[]{:S(2)}) %copy-start) | copy-done | bytes 194712
  3.4 0.0 copy-start.1
  3.4 0.7 %copy-done.1 = s32[16]{0:T(128)S(1)} copy-done((s32[16]{0:T(128)S(1)}, s32[16]{0:T(128)}, u32[]{:S(2)}) %copy-start.1) | copy-done | bytes 88
  4.1 0.0 copy-start.2
  4.1 0.7 %copy-done.2 = s32[16]{0:T(128)S(1)} copy-done((s32[16]{0:T(128)S(1)}, s32[16]{0:T(128)}, u32[]{:S(2)}) %copy-start.2) | copy-done | bytes 88
  4.7 15.6 %local_sums.1 = (bf16[4,8,80,640]{3,2,1,0:T(8,128)(2,1)S(1)}, bf16[4,80,384]{2,1,0:T(8,128)(2,1)S(1)}) custom-call(s32[16]{0:T(128)S(1)} %copy-done.1, s32[28,16]{1,0:T(8,128)S(1)} %copy.9.target_sector, s32[16]{0:T(128)S(1)} %copy-done.2, bf16[1,312,312]{2,1,0:T(8,128)(2,1)S(1)} %copy-done, bf16[28,312,312]{2,1,0:T(8,128)(2,1)} %bitcast.3, ...), custom_call_target="tpu_custom_call" | custom-call | tf_op jit(solution)/shard_map/local_sums/pallas_call | solution.py:403
  20.4 40.9 %reduce_pieces.1 = (bf16[4,78,312]{2,1,0:T(8,128)(2,1)S(1)}, f32[1,1]{1,0:T(1,128)}) custom-call(s32[16]{0:T(128)S(1)} %copy-done.1, s32[16]{0:T(128)S(1)} %copy-done.2, bf16[4,8,80,640]{3,2,1,0:T(8,128)(2,1)S(1)} %get-tuple-element.6.sums, bf16[4,80,384]{2,1,0:T(8,128)(2,1)S(1)} %get-tuple-element.7.live_pieces, f32[4,78,312]{2,1,0:T(8,128)S(1)} %copy.10.diagonal), custom_call_target="tpu_custom_call" | custom-call | tf_op jit(solution)/shard_map/reduce_pieces/pallas_call | solution.py:424
  61.2 0.8 %copy.11 = bf16[4,78,312]{2,0,1:T(4,128)(2,1)} copy(bf16[4,78,312]{2,1,0:T(8,128)(2,1)S(1)} %get-tuple-element.10) | data formatting | bytes 389376
Async XLA Ops:
  2.5 0.9 %copy-start = (bf16[1,312,312]{2,1,0:T(8,128)(2,1)S(1)}, bf16[1,312,312]{2,1,0:T(8,128)(2,1)}, u32[]{:S(2)}) copy-start(bf16[1,312,312]{2,1,0:T(8,128)(2,1)} %wave.1) | copy-start | bytes 584068
  3.4 0.7 %copy-start.1 = (s32[16]{0:T(128)S(1)}, s32[16]{0:T(128)}, u32[]{:S(2)}) copy-start(s32[16]{0:T(128)} %slot_sector.3) | copy-start | bytes 196
  4.1 0.7 %copy-start.2 = (s32[16]{0:T(128)S(1)}, s32[16]{0:T(128)}, u32[]{:S(2)}) copy-start(s32[16]{0:T(128)} %widths.3) | copy-start | bytes 196

commit v2 on v0

--- a/solution.py
+++ b/solution.py
@@ -1,9 +1,14 @@
+import functools
+
 import jax
 import jax.numpy as jnp
 from jax import lax
+from jax.experimental import pallas as pl
+from jax.experimental.pallas import tpu as pltpu
 from jax.sharding import PartitionSpec as P
 
 PIECES = 4
+MESH = pl.DeviceIdType.MESH
 
 
 def earlier_same(labels):
@@ -13,7 +18,7 @@
     return jnp.sum(jnp.logical_and(same_label, earlier).astype(jnp.int32), axis=-1)
 
 
-def shards(wavefunction, left_blocks, right_blocks, diagonal, target_sector, slot_sector, widths):
+def gathered_shards(wavefunction, left_blocks, right_blocks, diagonal, target_sector, slot_sector, widths):
     owners = lax.axis_size("sec")
     own_index = lax.axis_index("sec")
     term_count = left_blocks.shape[0]
@@ -102,6 +107,401 @@
     return (residual, jnp.reshape(quotient, (1,)))
 
 
+def round_up(value, unit):
+    return (value + unit - 1) // unit * unit
+
+
+def to_column(row, count):
+    wide = jnp.broadcast_to(row[:, :count], (count, count))
+    eye = lax.broadcasted_iota(jnp.int32, (count, count), 0) == lax.broadcasted_iota(
+        jnp.int32, (count, count), 1
+    )
+    return jnp.sum(jnp.where(eye, wide, 0.0), axis=1, keepdims=True)
+
+
+def make_plan(slot_row, target_rows, width_row, me):
+    owners, terms = target_rows.shape
+    slot_column = to_column(slot_row, owners)
+    at_owner = lax.broadcasted_iota(jnp.int32, (owners, 1), 0)
+    sector = jnp.sum(jnp.where(at_owner == me, slot_column, 0.0), axis=0, keepdims=True)
+    target = jnp.sum(
+        jnp.where(at_owner.astype(jnp.float32) == sector, target_rows, 0.0), axis=0, keepdims=True
+    )
+    owner_ids = at_owner.astype(jnp.float32)
+    slot = jnp.sum(jnp.where(slot_column == target, owner_ids, 0.0), axis=0, keepdims=True)
+    column = to_column(slot, terms)
+    term_row = lax.broadcasted_iota(jnp.int32, (terms, terms), 1)
+    term_column = lax.broadcasted_iota(jnp.int32, (terms, terms), 0)
+    ahead = jnp.logical_or(
+        slot < column, jnp.logical_and(slot == column, term_row < term_column)
+    )
+    rank = jnp.sum(jnp.where(ahead, 1.0, 0.0), axis=1, keepdims=True)
+    lanes = lax.broadcasted_iota(jnp.int32, (terms, 128), 1).astype(jnp.float32)
+    term_ids = lax.broadcasted_iota(jnp.int32, (terms, 128), 0).astype(jnp.float32)
+    order = jnp.sum(jnp.where(rank == lanes, term_ids, 0.0), axis=0, keepdims=True)
+    start = jnp.sum(jnp.where(column < lanes, 1.0, 0.0), axis=0, keepdims=True)
+    width_column = to_column(width_row, owners)
+    widths = jnp.sum(
+        jnp.where(owner_ids == slot_row, width_column, 0.0), axis=0, keepdims=True
+    )
+    return order, start, widths
+
+
+def fused_kernel(
+    slot_sector, target_sector, widths, wave, left, right, diagonal, residual, quotient,
+    slot_vmem, target_vmem, width_vmem, wave_vmem, plan_vmem, plan, lbuf, rbuf, running,
+    own, crecv, xrecv, zrecv, live_pieces, lives, diag_raw, product, stats, stats_all,
+    small_sem, plan_sem, lsem, rsem, diag_sem, self_sem,
+    csend_sem, crecv_sem, xsend_sem, xrecv_sem, zsend_sem, zrecv_sem,
+    lsend_sem, lrecv_sem, ssend_sem, srecv_sem,
+):
+    rep = lax.axis_index("rep")
+    me = lax.axis_index("sec")
+    owners = slot_sector.shape[1]
+    terms, width = lbuf.shape[0], lbuf.shape[1]
+    groups = owners // PIECES
+    capacity = (terms + groups) // groups
+    z, x, c = me // 4, (me // 2) % 2, me % 2
+    group = me % 4
+    units = 2 * PIECES
+    rows = width // PIECES
+    main = width // 128 * 128
+    rest = width - main
+    far, near = (1 - x) * 2, x * 2
+
+    small = [
+        pltpu.make_async_copy(source, target, small_sem.at[i])
+        for i, (source, target) in enumerate(
+            (
+                (wave.at[0], wave_vmem),
+                (slot_sector, slot_vmem),
+                (target_sector, target_vmem),
+                (widths, width_vmem),
+            )
+        )
+    ]
+    for copy in small:
+        copy.start()
+
+    @pl.loop(0, terms)
+    def _(t):
+        pltpu.make_async_copy(left.at[t], lbuf.at[t], lsem.at[t]).start()
+
+    @pl.loop(0, terms)
+    def _(t):
+        pltpu.make_async_copy(right.at[t], rbuf.at[t], rsem.at[t]).start()
+
+    diag_copy = pltpu.make_async_copy(diagonal, diag_raw, diag_sem)
+    diag_copy.start()
+
+    barrier = pltpu.get_barrier_semaphore()
+    for d in range(1, owners):
+        pl.semaphore_signal(
+            barrier, inc=1, device_id=(rep, (me + d) % owners), device_id_type=MESH
+        )
+
+    for copy in small:
+        copy.wait()
+    order, start, slot_widths = make_plan(
+        slot_vmem[...].astype(jnp.float32),
+        target_vmem[...].astype(jnp.float32),
+        width_vmem[...].astype(jnp.float32),
+        me,
+    )
+    plan_vmem[0:1, :] = order.astype(jnp.int32)
+    plan_vmem[1:2, :] = start.astype(jnp.int32)
+    plan_copy = pltpu.make_async_copy(plan_vmem, plan, plan_sem)
+    plan_copy.start()
+
+    def width_of(slot):
+        ids = lax.broadcasted_iota(jnp.int32, slot_widths.shape, 1)
+        picked = jnp.sum(jnp.where(ids == slot, slot_widths, 0.0), axis=1, keepdims=True)
+        return picked.astype(jnp.int32)
+
+    own_width = width_of(me)
+    row_ids = lax.broadcasted_iota(jnp.int32, (width, width), 0)
+    column_ids = lax.broadcasted_iota(jnp.int32, (width, width), 1)
+    keep = jnp.logical_and(row_ids < own_width, column_ids < own_width)
+    live_wide = jnp.where(keep, wave_vmem[...].astype(jnp.float32), 0.0)
+    live = live_wide.astype(jnp.bfloat16)
+    for p in range(PIECES):
+        piece = live_wide[p * rows : (p + 1) * rows].astype(jnp.bfloat16)
+        live_pieces[p, :rows, :width] = piece
+
+    def unit_of(i):
+        return ((z + 1 + i // 2) % PIECES) * 2 + i % 2
+
+    def core_copy(which, u):
+        return pltpu.make_async_remote_copy(
+            src_ref=own.at[2 * which, u], dst_ref=crecv.at[which, u],
+            send_sem=csend_sem.at[which, u], recv_sem=crecv_sem.at[which, u],
+            device_id=(rep, near + z * 4 + (1 - c)), device_id_type=MESH,
+        )
+
+    def x_copy(u):
+        return pltpu.make_async_remote_copy(
+            src_ref=own.at[1, u], dst_ref=xrecv.at[u],
+            send_sem=xsend_sem.at[u], recv_sem=xrecv_sem.at[u],
+            device_id=(rep, z * 4 + far + c), device_id_type=MESH,
+        )
+
+    def z_copy(u, source_z):
+        q = u % 2
+        return pltpu.make_async_remote_copy(
+            src_ref=own.at[3, u], dst_ref=zrecv.at[source_z, q],
+            send_sem=zsend_sem.at[u], recv_sem=zrecv_sem.at[source_z, q],
+            device_id=(rep, (u // 2) * 4 + group), device_id_type=MESH,
+        )
+
+    def live_copy(p, place):
+        return pltpu.make_async_remote_copy(
+            src_ref=live_pieces.at[p], dst_ref=lives.at[place],
+            send_sem=lsend_sem.at[p], recv_sem=lrecv_sem.at[place],
+            device_id=(rep, p * 4 + z), device_id_type=MESH,
+        )
+
+    def stats_copy(level, other, source):
+        device = z * 4 + other if level == 0 else other * 4 + group
+        return pltpu.make_async_remote_copy(
+            src_ref=stats.at[level], dst_ref=stats_all.at[level, source],
+            send_sem=ssend_sem.at[level, other], recv_sem=srecv_sem.at[level, source],
+            device_id=(rep, device), device_id_type=MESH,
+        )
+
+    batch = 4
+
+    @pl.loop(0, terms // batch)
+    def _(step):
+        for b in range(batch):
+            t = step * batch + b
+            pltpu.make_async_copy(left.at[t], lbuf.at[t], lsem.at[t]).wait()
+        for b in range(batch):
+            t = step * batch + b
+            half = jnp.dot(lbuf[t], live, preferred_element_type=jnp.float32)
+            lbuf[t] = half.astype(jnp.bfloat16)
+
+    pl.semaphore_wait(barrier, owners - 1)
+    self_copy = pltpu.make_async_copy(live_pieces.at[z], lives.at[group], self_sem)
+    for p in range(PIECES):
+
+        @pl.when(p * 4 + z != me)
+        def _():
+            live_copy(p, group).start()
+
+        @pl.when(p * 4 + z == me)
+        def _():
+            self_copy.start()
+
+    running[0] = jnp.zeros((width, width), jnp.float32)
+    plan_copy.wait()
+
+    @pl.loop(0, terms)
+    def _(t):
+        pltpu.make_async_copy(right.at[t], rbuf.at[t], rsem.at[t]).wait()
+
+    pad = jnp.zeros((rows, own.shape[-1] - 2 * width), jnp.float32)
+
+    @pl.loop(0, groups)
+    def _(k):
+        target_group = jnp.where(k < 2, far, near) + jnp.where(k % 2 == 0, 1 - c, c)
+        first = plan[1, target_group * PIECES]
+        for i in range(capacity):
+            t = jnp.clip(plan[0, jnp.clip(first + i, 0, terms - 1)], 0, terms - 1)
+            term = lax.dot_general(
+                lbuf[t], rbuf[t], (((1,), (1,)), ((), ())), preferred_element_type=jnp.float32
+            )
+            running[i + 1] = term if i == 0 else running[i] + term
+        for q in range(2):
+            ends = [
+                jnp.clip(plan[1, target_group * PIECES + 2 * q + e] - first, 0, capacity)
+                for e in range(3)
+            ]
+            for p in range(PIECES):
+                at = slice(p * rows, (p + 1) * rows)
+                low, middle, high = [running[end, at, :] for end in ends]
+                even, odd = middle - low, high - middle
+                packed = jnp.concatenate(
+                    [even[:, :main], odd[:, :main], even[:, main:], odd[:, main:], pad], axis=1
+                )
+                own[k, 2 * p + q, :rows, :] = packed.astype(own.dtype)
+
+        @pl.when(k % 2 == 0)
+        def _():
+            @pl.loop(0, units)
+            def _(i):
+                core_copy(k // 2, unit_of(i)).start()
+
+        @pl.when(k == 1)
+        def _():
+            @pl.loop(0, units)
+            def _(i):
+                u = unit_of(i)
+                core_copy(0, u).wait_recv()
+                total = own[1, u].astype(jnp.float32) + crecv[0, u].astype(jnp.float32)
+                own[1, u] = total.astype(own.dtype)
+                x_copy(u).start()
+
+    @pl.loop(0, units - 2)
+    def _(i):
+        u = unit_of(i)
+        core_copy(1, u).wait_recv()
+        x_copy(u).wait_recv()
+        total = own[3, u].astype(jnp.float32) + crecv[1, u].astype(jnp.float32)
+        total += xrecv[u].astype(jnp.float32)
+        own[3, u] = total.astype(own.dtype)
+        z_copy(u, z).start()
+
+    for j in range(PIECES):
+        source = group * 4 + j
+
+        @pl.when(source != me)
+        def _():
+            live_copy(0, j).wait_recv()
+
+        @pl.when(source == me)
+        def _():
+            self_copy.wait()
+
+    diag_copy.wait()
+    for j in range(PIECES):
+        product[j] = diag_raw[:, j, :] * lives[j, :rows, :width].astype(jnp.float32)
+
+    correlation = jnp.zeros((1, width), jnp.float32)
+    squares = jnp.zeros((1, width), jnp.float32)
+    for q in range(2):
+        u = z * 2 + q
+        core_copy(1, u).wait_recv()
+        x_copy(u).wait_recv()
+        total = own[3, u].astype(jnp.float32) + crecv[1, u].astype(jnp.float32)
+        total += xrecv[u].astype(jnp.float32)
+        for d in range(1, PIECES):
+            source_z = (z + d) % PIECES
+            z_copy(q, source_z).wait_recv()
+            total += zrecv[source_z, q].astype(jnp.float32)
+        total = total[:rows]
+        tail = 2 * main
+        for parity in range(2):
+            j = 2 * q + parity
+            applied = jnp.concatenate(
+                [
+                    total[:, parity * main : (parity + 1) * main],
+                    total[:, tail + parity * rest : tail + (parity + 1) * rest],
+                ],
+                axis=1,
+            )
+            live = lives[j, :rows, :width].astype(jnp.float32)
+            block = product[j] + applied
+            product[j] = block
+            correlation += jnp.sum(live * block, axis=0, keepdims=True)
+            squares += jnp.sum(live * live, axis=0, keepdims=True)
+
+    row_ids = lax.broadcasted_iota(jnp.int32, stats.shape[1:], 0)
+    mine = jnp.where(row_ids == 0, jnp.sum(correlation), jnp.sum(squares))
+    for level in range(2):
+        here = group if level == 0 else z
+        stats[level] = mine
+        stats_all[level, here] = mine
+        for d in range(1, PIECES):
+            stats_copy(level, (here + d) % PIECES, here).start()
+        for d in range(1, PIECES):
+            stats_copy(level, here, (here + d) % PIECES).wait_recv()
+        mine = stats_all[level, 0]
+        for d in range(1, PIECES):
+            mine += stats_all[level, d]
+
+    ratio = mine[0:1, 0:1] / mine[1:2, 0:1]
+    quotient[...] = jnp.broadcast_to(ratio, quotient.shape)
+    row_ids = lax.broadcasted_iota(jnp.int32, (rows, width), 0) + z * rows
+    column_ids = lax.broadcasted_iota(jnp.int32, (rows, width), 1)
+    for j in range(PIECES):
+        slot_width = width_of(group * 4 + j)
+        keep = jnp.logical_and(row_ids < slot_width, column_ids < slot_width)
+        live = lives[j, :rows, :width].astype(jnp.float32)
+        value = jnp.where(keep, product[j] - ratio * live, 0.0)
+        residual[j] = value.astype(residual.dtype)
+
+    @pl.loop(0, units)
+    def _(u):
+        core_copy(0, u).wait_send()
+        core_copy(1, u).wait_send()
+        x_copy(u).wait_send()
+
+    @pl.loop(0, units - 2)
+    def _(i):
+        z_copy(unit_of(i), z).wait_send()
+
+    for p in range(PIECES):
+
+        @pl.when(p * 4 + z != me)
+        def _():
+            live_copy(p, group).wait_send()
+
+    for level in range(2):
+        here = group if level == 0 else z
+        for d in range(1, PIECES):
+            stats_copy(level, (here + d) % PIECES, here).wait_send()
+
+
+def kernel_shards(
+    wavefunction, left_blocks, right_blocks, diagonal, target_sector, slot_sector, widths
+):
+    terms, _, width, _ = left_blocks.shape
+    owners = slot_sector.shape[0]
+    rows = width // PIECES
+    groups = owners // PIECES
+    capacity = (terms + groups) // groups
+    units = 2 * PIECES
+    tall = round_up(rows, 16)
+    lanes = round_up(width, 128)
+    block = (tall, round_up(2 * width, 128))
+    vmem = pl.BlockSpec(memory_space=pltpu.VMEM)
+    hbm = pl.BlockSpec(memory_space=pl.ANY)
+    dma = pltpu.SemaphoreType.DMA
+    wide = jnp.bfloat16
+    residual, quotient = pl.pallas_call(
+        fused_kernel,
+        out_shape=(
+            jax.ShapeDtypeStruct((PIECES, rows, width), jnp.bfloat16),
+            jax.ShapeDtypeStruct((1, 1), jnp.float32),
+        ),
+        in_specs=[hbm] * 7,
+        out_specs=(vmem, vmem),
+        scratch_shapes=[
+            pltpu.VMEM((1, owners), jnp.int32),
+            pltpu.VMEM((owners, terms), jnp.int32),
+            pltpu.VMEM((1, owners), jnp.int32),
+            pltpu.VMEM((width, width), wide),
+            pltpu.VMEM((8, 128), jnp.int32),
+            pltpu.SMEM((8, 128), jnp.int32),
+            pltpu.VMEM((terms, width, width), wide),
+            pltpu.VMEM((terms, width, width), wide),
+            pltpu.VMEM((capacity + 1, width, width), jnp.float32),
+            pltpu.VMEM((4, units, *block), wide),
+            pltpu.VMEM((2, units, *block), wide),
+            pltpu.VMEM((units, *block), wide),
+            pltpu.VMEM((PIECES, 2, *block), wide),
+            pltpu.VMEM((PIECES, tall, lanes), wide),
+            pltpu.VMEM((PIECES, tall, lanes), wide),
+            pltpu.VMEM((rows, PIECES, width), jnp.float32),
+            pltpu.VMEM((PIECES, rows, width), jnp.float32),
+            pltpu.VMEM((2, 8, 128), jnp.float32),
+            pltpu.VMEM((2, PIECES, 8, 128), jnp.float32),
+            dma((4,)), dma, dma((terms,)), dma((terms,)), dma, dma,
+            dma((2, units)), dma((2, units)), dma((units,)), dma((units,)),
+            dma((units,)), dma((PIECES, 2)),
+            dma((PIECES,)), dma((PIECES,)), dma((2, PIECES)), dma((2, PIECES)),
+        ],
+        compiler_params=pltpu.CompilerParams(
+            collective_id=0, has_side_effects=True, vmem_limit_bytes=58 << 20
+        ),
+        name="fused",
+    )(
+        slot_sector[None], target_sector.T, widths[None], wavefunction,
+        left_blocks[:, 0], right_blocks[:, 0], jnp.transpose(diagonal, (1, 0, 2)),
+    )
+    return residual, jnp.reshape(quotient, (1,))
+
+
 def solution(mesh):
     in_specs = (
         P(("rep", "sec"), None, None),
@@ -113,4 +513,6 @@
         P("rep"),
     )
     out_specs = (P(("rep", "sec"), None, None), P("rep"))
+    fast = mesh.shape["sec"] == PIECES * 4
+    shards = kernel_shards if fast else gathered_shards
     return jax.shard_map(shards, mesh=mesh, in_specs=in_specs, out_specs=out_specs, check_vma=False)

time: 298 us -> 51.4 us (0.17)
  waiting for transfers between devices: 136 us -> 0 us
  blocking collectives: 62.2 us -> 0 us
  local copies, waits for them, and re-layouts: 53.5 us -> 1.73 us
  Pallas kernels: 0 us -> 47.1 us
  matrix products: 23.4 us -> 0 us
  other arithmetic: 11 us -> 0 us
  starting transfers between devices: 7.39 us -> 0 us
    all_to_all x1 -> x0, waiting for transfers between devices: 136 us -> none  [shards(): lax.all_to_all(outgoing, 'sec', split_axis=0, concat_axis=0, tiled=True)]
    psum x1 -> x0, blocking collectives: 62.2 us -> none  [shards(): lax.psum((correlation_local, jnp.sum(live_pieces * live_pieces)), 'sec')]
    pallas_call x0 -> x1, Pallas kernels: none -> 47.1 us  [kernel_shards(): pl.pallas_call(fused_kernel, out_shape=(jax.ShapeDtypeStruct((PIECES, row...]
    scatter x3 -> x0, local copies, waits for them, and re-layouts: 33 us -> none  [the longest x2 32.4 us: shards(): outgoing = jnp.zeros((owners, capacity, piece_rows, block_width), jnp.bfl...]
    dot_general x3 -> x0, matrix products: 23.4 us -> none  [the longest x1 13.6 us: shards(): jnp.einsum('tik,tlk->til', half_done, right_blocks[:, 0], preferred_eleme...]
    concatenate x3 -> x0, local copies, waits for them, and re-layouts: 10.2 us -> none  [the longest x2 10.1 us: shards(): jnp.concatenate([live_block[None], term_blocks])]
    all_to_all x1 -> x0, starting transfers between devices: 7.39 us -> none  [shards(): lax.all_to_all(outgoing, 'sec', split_axis=0, concat_axis=0, tiled=True)]
    concatenate x2 -> x0, other arithmetic: 7.27 us -> none  [the longest x1 7.18 us: shards(): jnp.concatenate([live_block[None], term_blocks])]
  transfers between devices with their start and end apart: 1 -> 0, of which waited for: 1 -> 0; matrix products, arithmetic and copies ran while one was open for 1% -> 0% of each run, Pallas kernels for 0% -> 0%
where the time goes in v2:
time: 51.4 us; the launch traced here: 51.2 us
  Pallas kernels  47.1 us (92%)
  between operations  2.39 us (5%)
  local copies, waits for them, and re-layouts  1.73 us (3%)
    pallas_call x1, Pallas kernels, kernel_shards(): pl.pallas_call(fused_kernel, out_shape=(jax.ShapeDtypeStruct((PIECES, row...  47.1 us
    unnamed x1, local copies, waits for them, and re-layouts  1.73 us

profile of v2, /device:TPU:0, one launch (start us, length us, event | category | flops | bytes accessed | tf_op | source)
XLA Modules:
  0.0 51.2 jit_solution(13611067284574971887)
XLA Ops:
  0.6 47.1 %fused.1 = (bf16[4,78,312]{2,1,0:T(8,128)(2,1)}, f32[1,1]{1,0:T(1,128)}) custom-call(s32[1,16]{1,0:T(1,128)} %bitcast.11, s32[16,28]{1,0:T(8,128)} %bitcast.10, s32[1,16]{1,0:T(1,128)} %bitcast.12, bf16[1,312,312]{2,1,0:T(8,128)(2,1)} %wave.1, bf16[28,312,312]{2,1,0:T(8,128)(2,1)} %bitcast.7, bf16[28,312,312]{2,1,0:T(8,128)(2,1)} %bitcast.8, ...), custom_call_target="tpu_custom_call" | custom-call | tf_op jit(solution)/shard_map/fused/pallas_call | solution.py:461
  47.7 1.7 %copy.9 = bf16[4,78,312]{2,0,1:T(4,128)(2,1)} copy(bf16[4,78,312]{2,1,0:T(8,128)(2,1)} %get-tuple-element.6) | data formatting | bytes 389376

commit v3 on v2

--- a/solution.py
+++ b/solution.py
@@ -197,7 +197,7 @@
     barrier = pltpu.get_barrier_semaphore()
     for d in range(1, owners):
         pl.semaphore_signal(
-            barrier, inc=1, device_id=(rep, (me + d) % owners), device_id_type=MESH
+            barrier, inc=1, device_id=(rep, me ^ d), device_id_type=MESH
         )
 
     for copy in small:
@@ -229,7 +229,9 @@
         live_pieces[p, :rows, :width] = piece
 
     def unit_of(i):
-        return ((z + 1 + i // 2) % PIECES) * 2 + i % 2
+        hop = i // 2
+        far_first = jnp.where(hop < 2, 2 + hop, 3 - hop)
+        return (z ^ far_first) * 2 + i % 2
 
     def core_copy(which, u):
         return pltpu.make_async_remote_copy(
@@ -260,12 +262,11 @@
             device_id=(rep, p * 4 + z), device_id_type=MESH,
         )
 
-    def stats_copy(level, other, source):
-        device = z * 4 + other if level == 0 else other * 4 + group
+    def stats_copy(other, source):
         return pltpu.make_async_remote_copy(
-            src_ref=stats.at[level], dst_ref=stats_all.at[level, source],
-            send_sem=ssend_sem.at[level, other], recv_sem=srecv_sem.at[level, source],
-            device_id=(rep, device), device_id_type=MESH,
+            src_ref=stats, dst_ref=stats_all.at[source],
+            send_sem=ssend_sem.at[other], recv_sem=srecv_sem.at[source],
+            device_id=(rep, other), device_id_type=MESH,
         )
 
     batch = 4
@@ -395,19 +396,17 @@
             correlation += jnp.sum(live * block, axis=0, keepdims=True)
             squares += jnp.sum(live * live, axis=0, keepdims=True)
 
-    row_ids = lax.broadcasted_iota(jnp.int32, stats.shape[1:], 0)
+    row_ids = lax.broadcasted_iota(jnp.int32, stats.shape, 0)
     mine = jnp.where(row_ids == 0, jnp.sum(correlation), jnp.sum(squares))
-    for level in range(2):
-        here = group if level == 0 else z
-        stats[level] = mine
-        stats_all[level, here] = mine
-        for d in range(1, PIECES):
-            stats_copy(level, (here + d) % PIECES, here).start()
-        for d in range(1, PIECES):
-            stats_copy(level, here, (here + d) % PIECES).wait_recv()
-        mine = stats_all[level, 0]
-        for d in range(1, PIECES):
-            mine += stats_all[level, d]
+    stats[...] = mine
+    stats_all[me] = mine
+    for d in range(owners - 1, 0, -1):
+        stats_copy(me ^ d, me).start()
+    for d in range(1, owners):
+        stats_copy(me, me ^ d).wait_recv()
+    mine = stats_all[0]
+    for d in range(1, owners):
+        mine += stats_all[d]
 
     ratio = mine[0:1, 0:1] / mine[1:2, 0:1]
     quotient[...] = jnp.broadcast_to(ratio, quotient.shape)
@@ -436,10 +435,8 @@
         def _():
             live_copy(p, group).wait_send()
 
-    for level in range(2):
-        here = group if level == 0 else z
-        for d in range(1, PIECES):
-            stats_copy(level, (here + d) % PIECES, here).wait_send()
+    for d in range(1, owners):
+        stats_copy(me ^ d, me).wait_send()
 
 
 def kernel_shards(
@@ -484,12 +481,12 @@
             pltpu.VMEM((PIECES, tall, lanes), wide),
             pltpu.VMEM((rows, PIECES, width), jnp.float32),
             pltpu.VMEM((PIECES, rows, width), jnp.float32),
-            pltpu.VMEM((2, 8, 128), jnp.float32),
-            pltpu.VMEM((2, PIECES, 8, 128), jnp.float32),
+            pltpu.VMEM((8, 128), jnp.float32),
+            pltpu.VMEM((owners, 8, 128), jnp.float32),
             dma((4,)), dma, dma((terms,)), dma((terms,)), dma, dma,
             dma((2, units)), dma((2, units)), dma((units,)), dma((units,)),
             dma((units,)), dma((PIECES, 2)),
-            dma((PIECES,)), dma((PIECES,)), dma((2, PIECES)), dma((2, PIECES)),
+            dma((PIECES,)), dma((PIECES,)), dma((owners,)), dma((owners,)),
         ],
         compiler_params=pltpu.CompilerParams(
             collective_id=0, has_side_effects=True, vmem_limit_bytes=58 << 20

time: 51.4 us -> 48.6 us (0.946)
  Pallas kernels: 47.1 us -> 44.3 us
    pallas_call x1, Pallas kernels: 47.1 us -> 44.3 us  [kernel_shards(): pl.pallas_call(fused_kernel, out_shape=(jax.ShapeDtypeStruct((PIECES, row...]
where the time goes in v3:
time: 48.6 us; the launch traced here: 48.4 us
  Pallas kernels  44.3 us (91%)
  between operations  2.39 us (5%)
  local copies, waits for them, and re-layouts  1.73 us (4%)
    pallas_call x1, Pallas kernels, kernel_shards(): pl.pallas_call(fused_kernel, out_shape=(jax.ShapeDtypeStruct((PIECES, row...  44.3 us
    unnamed x1, local copies, waits for them, and re-layouts  1.73 us

profile of v3, /device:TPU:0, one launch (start us, length us, event | category | flops | bytes accessed | tf_op | source)
XLA Modules:
  0.0 48.4 jit_solution(16637812144596790456)
XLA Ops:
  0.6 44.3 %fused.1 = (bf16[4,78,312]{2,1,0:T(8,128)(2,1)}, f32[1,1]{1,0:T(1,128)}) custom-call(s32[1,16]{1,0:T(1,128)} %bitcast.11, s32[16,28]{1,0:T(8,128)} %bitcast.10, s32[1,16]{1,0:T(1,128)} %bitcast.12, bf16[1,312,312]{2,1,0:T(8,128)(2,1)} %wave.1, bf16[28,312,312]{2,1,0:T(8,128)(2,1)} %bitcast.7, bf16[28,312,312]{2,1,0:T(8,128)(2,1)} %bitcast.8, ...), custom_call_target="tpu_custom_call" | custom-call | tf_op jit(solution)/shard_map/fused/pallas_call | solution.py:458
  45.0 1.7 %copy.9 = bf16[4,78,312]{2,0,1:T(4,128)(2,1)} copy(bf16[4,78,312]{2,1,0:T(8,128)(2,1)} %get-tuple-element.6) | data formatting | bytes 389376

commit v4 on v3

--- a/solution.py
+++ b/solution.py
@@ -230,8 +230,8 @@
 
     def unit_of(i):
         hop = i // 2
-        far_first = jnp.where(hop < 2, 2 + hop, 3 - hop)
-        return (z ^ far_first) * 2 + i % 2
+        away = jnp.where(hop == 0, 3, jnp.where(hop == 1, 1, jnp.where(hop == 2, 2, 0)))
+        return (z ^ away) * 2 + i % 2
 
     def core_copy(which, u):
         return pltpu.make_async_remote_copy(
@@ -247,12 +247,13 @@
             device_id=(rep, z * 4 + far + c), device_id_type=MESH,
         )
 
-    def z_copy(u, source_z):
-        q = u % 2
+    def z_copy(i):
+        hop, q = i // 2, i % 2
+        target = z ^ jnp.where(hop < 2, 1, 2)
         return pltpu.make_async_remote_copy(
-            src_ref=own.at[3, u], dst_ref=zrecv.at[source_z, q],
-            send_sem=zsend_sem.at[u], recv_sem=zrecv_sem.at[source_z, q],
-            device_id=(rep, (u // 2) * 4 + group), device_id_type=MESH,
+            src_ref=own.at[3, unit_of(i)], dst_ref=zrecv.at[hop, q],
+            send_sem=zsend_sem.at[hop, q], recv_sem=zrecv_sem.at[hop, q],
+            device_id=(rep, target * 4 + group), device_id_type=MESH,
         )
 
     def live_copy(p, place):
@@ -342,15 +343,26 @@
                 own[1, u] = total.astype(own.dtype)
                 x_copy(u).start()
 
-    @pl.loop(0, units - 2)
-    def _(i):
-        u = unit_of(i)
+    def near_total(u):
         core_copy(1, u).wait_recv()
         x_copy(u).wait_recv()
         total = own[3, u].astype(jnp.float32) + crecv[1, u].astype(jnp.float32)
-        total += xrecv[u].astype(jnp.float32)
+        return total + xrecv[u].astype(jnp.float32)
+
+    @pl.loop(0, 4)
+    def _(i):
+        u = unit_of(i)
+        own[3, u] = near_total(u).astype(own.dtype)
+        z_copy(i).start()
+
+    @pl.loop(4, 6)
+    def _(i):
+        u = unit_of(i)
+        total = near_total(u)
+        z_copy(i - 4).wait_recv()
+        total += zrecv[0, i - 4].astype(jnp.float32)
         own[3, u] = total.astype(own.dtype)
-        z_copy(u, z).start()
+        z_copy(i).start()
 
     for j in range(PIECES):
         source = group * 4 + j
@@ -371,14 +383,10 @@
     squares = jnp.zeros((1, width), jnp.float32)
     for q in range(2):
         u = z * 2 + q
-        core_copy(1, u).wait_recv()
-        x_copy(u).wait_recv()
-        total = own[3, u].astype(jnp.float32) + crecv[1, u].astype(jnp.float32)
-        total += xrecv[u].astype(jnp.float32)
-        for d in range(1, PIECES):
-            source_z = (z + d) % PIECES
-            z_copy(q, source_z).wait_recv()
-            total += zrecv[source_z, q].astype(jnp.float32)
+        total = near_total(u)
+        for hop in range(1, 3):
+            z_copy(2 * hop + q).wait_recv()
+            total += zrecv[hop, q].astype(jnp.float32)
         total = total[:rows]
         tail = 2 * main
         for parity in range(2):
@@ -427,7 +435,7 @@
 
     @pl.loop(0, units - 2)
     def _(i):
-        z_copy(unit_of(i), z).wait_send()
+        z_copy(i).wait_send()
 
     for p in range(PIECES):
 
@@ -476,7 +484,7 @@
             pltpu.VMEM((4, units, *block), wide),
             pltpu.VMEM((2, units, *block), wide),
             pltpu.VMEM((units, *block), wide),
-            pltpu.VMEM((PIECES, 2, *block), wide),
+            pltpu.VMEM((3, 2, *block), wide),
             pltpu.VMEM((PIECES, tall, lanes), wide),
             pltpu.VMEM((PIECES, tall, lanes), wide),
             pltpu.VMEM((rows, PIECES, width), jnp.float32),
@@ -485,7 +493,7 @@
             pltpu.VMEM((owners, 8, 128), jnp.float32),
             dma((4,)), dma, dma((terms,)), dma((terms,)), dma, dma,
             dma((2, units)), dma((2, units)), dma((units,)), dma((units,)),
-            dma((units,)), dma((PIECES, 2)),
+            dma((3, 2)), dma((3, 2)),
             dma((PIECES,)), dma((PIECES,)), dma((owners,)), dma((owners,)),
         ],
         compiler_params=pltpu.CompilerParams(

time: 48.6 us -> 48.7 us (level)
  no operation moved by 1% of the time
where the time goes in v4:
time: 48.7 us; the launch traced here: 48.5 us
  Pallas kernels  44.4 us (91%)
  between operations  2.39 us (5%)
  local copies, waits for them, and re-layouts  1.73 us (4%)
    pallas_call x1, Pallas kernels, kernel_shards(): pl.pallas_call(fused_kernel, out_shape=(jax.ShapeDtypeStruct((PIECES, row...  44.4 us
    unnamed x1, local copies, waits for them, and re-layouts  1.73 us

profile of v4, /device:TPU:0, one launch (start us, length us, event | category | flops | bytes accessed | tf_op | source)
XLA Modules:
  0.0 48.5 jit_solution(14424810442922822959)
XLA Ops:
  0.6 44.4 %fused.1 = (bf16[4,78,312]{2,1,0:T(8,128)(2,1)}, f32[1,1]{1,0:T(1,128)}) custom-call(s32[1,16]{1,0:T(1,128)} %bitcast.11, s32[16,28]{1,0:T(8,128)} %bitcast.10, s32[1,16]{1,0:T(1,128)} %bitcast.12, bf16[1,312,312]{2,1,0:T(8,128)(2,1)} %wave.1, bf16[28,312,312]{2,1,0:T(8,128)(2,1)} %bitcast.7, bf16[28,312,312]{2,1,0:T(8,128)(2,1)} %bitcast.8, ...), custom_call_target="tpu_custom_call" | custom-call | tf_op jit(solution)/shard_map/fused/pallas_call | solution.py:466
  45.1 1.7 %copy.9 = bf16[4,78,312]{2,0,1:T(4,128)(2,1)} copy(bf16[4,78,312]{2,1,0:T(8,128)(2,1)} %get-tuple-element.6) | data formatting | bytes 389376
